TPU v7x, 32 devices: a whole 2x2x4 slice. The times are simulated.
32 devices in a mesh: replica: 2 (over x), req: 8 (over z, y), tp: 2 (over core).
Axes of the slice: x: 2, y: 2, z: 4, core: 2. Of those that a mesh axis runs over, the one named last changes fastest.
Arguments:
- normed_hidden_rows: bfloat16 [2048, 4096], P(('replica', 'req')), parts along dimension 0, may hold values from -30 to 30
- base_query_rows: bfloat16 [2048, 2048], P(('replica', 'req'), 'tp'), parts along dimension 0, may hold values from -20 to 20
- incoming_key: bfloat16 [2048, 2048], P(('replica', 'req'), 'tp'), parts along dimension 0, may hold values from -8 to 8
- base_value_rows: bfloat16 [2048, 2048], P(('replica', 'req'), 'tp'), parts along dimension 0, may hold values from -3 to 3
- stored_keys: bfloat16 [2048, 16, 2048], P(('replica', 'req'), None, 'tp'), parts along dimension 0, may hold values from -20 to 20
- stored_values: bfloat16 [2048, 16, 2048], P(('replica', 'req'), None, 'tp'), parts along dimension 0, may hold values from -3 to 3
- cache_fill_length: int32 [2048], P(('replica', 'req')), parts along dimension 0, may hold values from 2 to 16, as said below
- adapter_of_row: int32 [2048], P(('replica', 'req')), parts along dimension 0, may hold values from 0 to 127, as said below
- adapter_pool_row: int32 [256], P('replica'), parts along dimension 0, may hold values from 0 to 127, as said below
- output_projection_weight: bfloat16 [2048, 4096], P('tp'), may hold values from -0.125 to 0.125
- output_block_scales: float32 [16, 32], P('tp'), may hold values from 0.5 to 2
- query_value_down_maps: bfloat16 [128, 32, 4096], P('req'), may hold values from -0.09375 to 0.09375
- query_value_up_maps: bfloat16 [128, 32, 2048], P('req', None, 'tp'), may hold values from -1.5 to 1.5
- output_down_maps: bfloat16 [128, 16, 2048], P('req', None, 'tp'), may hold values from -0.125 to 0.125
- output_up_maps: bfloat16 [128, 16, 4096], P('req', None, 'tp'), may hold values from -1.5 to 1.5
Outputs:
- layer_out: bfloat16 [2048, 4096], P(('replica', 'req'), 'tp'), parts along dimension 0
There are 2 independent parts, one for each index of `replica`. A program takes and returns all parts, laid end to end along the dimension named above; an argument that names none is the same for every part. Nothing has to cross between parts.
Inputs may be any that keep to these rules, and one draw needn't show every extreme that they name: A permutation: adapter a is stored at row adapter_pool_row[a] of every adapter array. `adapter_of_row`: the rows of one device name adapters stored on one request shard (adapter_pool_row[id] // 16) at most 32 times; on every device some shard is named exactly 32 times. `cache_fill_length`: on every device some row has all 16 positions filled.
All inputs are finite; a program needn't handle non-finite values.
Results may differ from a plain program's by a relative error of at most 0.015.
Values may be sent and summed in bfloat16 or wider, within the bound.
A program may use at most 128 MiB of HBM per device.

v0:
```python
import math

import jax
import jax.numpy as jnp
from jax import lax
from jax.sharding import PartitionSpec as P

HEAD_DIM = 128
ADAPTER_RANK = 16
BLOCK = 128


adapter_scale = 2.0


def locate(adapter_of_row, adapter_pool_row, owners, adapter_spread, capacity):
    table_index = jnp.arange(adapter_pool_row.shape[0], dtype=jnp.int32)
    slot_index = jnp.sum(
        jnp.where(adapter_of_row[:, None] == table_index[None, :], adapter_pool_row[None, :], 0),
        axis=1,
    )
    owner = slot_index // adapter_spread
    local_slot = slot_index % adapter_spread
    row_count = adapter_of_row.shape[0]
    row_index = jnp.arange(row_count, dtype=jnp.int32)
    earlier = (owner[:, None] == owner[None, :]) & (row_index[None, :] < row_index[:, None])
    rank_in = jnp.sum(earlier.astype(jnp.int32), axis=1)
    place_index = owner * capacity + rank_in
    placing = place_index[:, None] == jnp.arange(owners * capacity, dtype=jnp.int32)[None, :]
    slots_buf = jnp.sum(jnp.where(placing, local_slot[:, None] + 1, 0), axis=0) - 1
    return (placing.astype(jnp.bfloat16), slots_buf.reshape(owners, capacity))


def select_shrink(shrink_all, slots_in, adapter_spread):
    chosen = (slots_in[:, None] == jnp.arange(adapter_spread, dtype=jnp.int32)[None, :]).astype(
        jnp.float32
    )
    return (jnp.sum(shrink_all * chosen[:, :, None], axis=1), chosen)


def qv_owner(received, down_map_table, up_map_table):
    rows_in, slots_in = received
    owners, pieces, features = rows_in.shape
    adapter_spread = down_map_table.shape[0]
    flat_rows = rows_in.reshape(owners * pieces, features)
    shrink_all = jnp.einsum(
        "md,ajd->maj", flat_rows, down_map_table, preferred_element_type=jnp.float32
    )
    rank_projection, chosen = select_shrink(
        shrink_all, slots_in.reshape(owners * pieces), adapter_spread
    )
    rank_projection = lax.psum(rank_projection, "tp")
    rank_projection = rank_projection.astype(jnp.bfloat16)
    mixed_rows = chosen.astype(jnp.bfloat16)[:, :, None] * rank_projection[:, None, :]
    head_width = up_map_table.shape[2]
    mixed_query = mixed_rows[:, :, :ADAPTER_RANK].reshape(
        owners * pieces, adapter_spread * ADAPTER_RANK
    )
    mixed_value = mixed_rows[:, :, ADAPTER_RANK:].reshape(
        owners * pieces, adapter_spread * ADAPTER_RANK
    )
    up_query = up_map_table[:, :ADAPTER_RANK, :].reshape(adapter_spread * ADAPTER_RANK, head_width)
    up_value = up_map_table[:, ADAPTER_RANK:, :].reshape(adapter_spread * ADAPTER_RANK, head_width)
    query_correction = jnp.dot(mixed_query, up_query, preferred_element_type=jnp.float32)
    value_correction = jnp.dot(mixed_value, up_value, preferred_element_type=jnp.float32)
    adapter_corrections = (
        adapter_scale * jnp.concatenate([query_correction, value_correction], axis=1)
    ).astype(jnp.bfloat16)
    return lax.all_to_all(
        adapter_corrections.reshape(owners, pieces, 2 * head_width),
        "req",
        split_axis=0,
        concat_axis=0,
        tiled=True,
    )


def o_owner(received, down_map_table, up_map_table):
    context_in, slots_in = received
    owners, pieces, features = context_in.shape
    adapter_spread = down_map_table.shape[0]
    flat_rows = context_in.reshape(owners * pieces, features)
    shrink_all = jnp.einsum(
        "mk,ajk->maj", flat_rows, down_map_table, preferred_element_type=jnp.float32
    )
    rank_projection, chosen = select_shrink(
        shrink_all, slots_in.reshape(owners * pieces), adapter_spread
    )
    rank_projection = lax.psum(rank_projection, "tp").astype(jnp.bfloat16)
    mixed_rows = (chosen.astype(jnp.bfloat16)[:, :, None] * rank_projection[:, None, :]).reshape(
        owners * pieces, adapter_spread * ADAPTER_RANK
    )
    out_width = up_map_table.shape[2]
    output_correction = jnp.dot(
        mixed_rows,
        up_map_table.reshape(adapter_spread * ADAPTER_RANK, out_width),
        preferred_element_type=jnp.float32,
    )
    output_correction = (adapter_scale * output_correction).astype(jnp.bfloat16)
    return lax.all_to_all(
        output_correction.reshape(owners, pieces, out_width),
        "req",
        split_axis=0,
        concat_axis=0,
        tiled=True,
    )


def attend(query_rows, incoming_key, value_new, stored_keys, stored_values, cache_fill_length):
    row_count, cache_len, head_width = stored_keys.shape
    heads_dev = head_width // HEAD_DIM
    inverse_root = 1.0 / math.sqrt(HEAD_DIM)
    query_heads = query_rows.reshape(row_count, heads_dev, HEAD_DIM)
    keys_heads = stored_keys.reshape(row_count, cache_len, heads_dev, HEAD_DIM)
    values_heads = stored_values.reshape(row_count, cache_len, heads_dev, HEAD_DIM)
    new_keys = incoming_key.reshape(row_count, heads_dev, HEAD_DIM)
    new_values = value_new.reshape(row_count, heads_dev, HEAD_DIM)
    scores = (
        jnp.einsum("rhd,rphd->rhp", query_heads, keys_heads, preferred_element_type=jnp.float32)
        * inverse_root
    )
    own_score = (
        jnp.einsum("rhd,rhd->rh", query_heads, new_keys, preferred_element_type=jnp.float32)
        * inverse_root
    )
    usable = jnp.arange(cache_len, dtype=jnp.int32)[None, :] < cache_fill_length[:, None]
    scores = jnp.where(usable[:, None, :], scores, -jnp.inf)
    highest = jnp.maximum(jnp.max(scores, axis=-1), own_score)
    cache_exp = jnp.exp(scores - highest[:, :, None])
    own_exp = jnp.exp(own_score - highest)
    denominator = jnp.sum(cache_exp, axis=-1) + own_exp
    weights = (cache_exp / denominator[:, :, None]).astype(jnp.bfloat16)
    own_weight = (own_exp / denominator).astype(jnp.bfloat16)
    context = jnp.einsum("rhp,rphd->rhd", weights, values_heads, preferred_element_type=jnp.float32)
    context = context + own_weight.astype(jnp.float32)[:, :, None] * new_values.astype(jnp.float32)
    return context.astype(jnp.bfloat16).reshape(row_count, head_width)


def block_product(context, output_projection_weight, output_block_scales):
    row_count = context.shape[0]
    in_blocks, out_blocks = output_block_scales.shape
    context_blocks = context.reshape(row_count, in_blocks, BLOCK)
    weight_blocks = output_projection_weight.reshape(in_blocks, BLOCK, out_blocks, BLOCK)
    partial_terms = jnp.einsum(
        "rkc,kcnd->rknd", context_blocks, weight_blocks, preferred_element_type=jnp.float32
    )
    scaled = jnp.sum(partial_terms * output_block_scales[None, :, :, None], axis=1)
    return scaled.reshape(row_count, out_blocks * BLOCK)


def shards(
    normed_hidden_rows,
    base_query_rows,
    incoming_key,
    base_value_rows,
    stored_keys,
    stored_values,
    cache_fill_length,
    adapter_of_row,
    adapter_pool_row,
    output_projection_weight,
    output_block_scales,
    query_value_down_maps,
    query_value_up_maps,
    output_down_maps,
    output_up_maps,
):
    owners = lax.axis_size("req")
    adapter_spread = query_value_down_maps.shape[0]
    row_count = adapter_of_row.shape[0]
    capacity = max(2, 2 * ((row_count + owners - 1) // owners))
    placing, slots_buf = locate(adapter_of_row, adapter_pool_row, owners, adapter_spread, capacity)

    def pack_rows(values):
        packed = jnp.einsum(
            "rs,rf->sf", placing, values, preferred_element_type=jnp.float32
        ).astype(values.dtype)
        return packed.reshape(owners, capacity, values.shape[1])

    def unpack_rows(returned):
        return jnp.dot(
            placing,
            returned.reshape(owners * capacity, returned.shape[2]),
            preferred_element_type=jnp.float32,
        )

    half_width = normed_hidden_rows.shape[1] // lax.axis_size("tp")
    offset = lax.axis_index("tp") * half_width
    part_rows = lax.dynamic_slice_in_dim(normed_hidden_rows, offset, half_width, 1)
    part_down = lax.dynamic_slice_in_dim(query_value_down_maps, offset, half_width, 2)
    returned = qv_owner(
        (
            lax.all_to_all(pack_rows(part_rows), "req", split_axis=0, concat_axis=0, tiled=True),
            lax.all_to_all(slots_buf, "req", split_axis=0, concat_axis=0, tiled=True),
        ),
        down_map_table=part_down,
        up_map_table=query_value_up_maps,
    )
    adapter_corrections = unpack_rows(returned)
    head_width = base_query_rows.shape[1]
    query_rows = (base_query_rows.astype(jnp.float32) + adapter_corrections[:, :head_width]).astype(
        jnp.bfloat16
    )
    value_new = (base_value_rows.astype(jnp.float32) + adapter_corrections[:, head_width:]).astype(
        jnp.bfloat16
    )
    context = attend(
        query_rows, incoming_key, value_new, stored_keys, stored_values, cache_fill_length
    )
    returned_o = o_owner(
        (
            lax.all_to_all(pack_rows(context), "req", split_axis=0, concat_axis=0, tiled=True),
            lax.all_to_all(slots_buf, "req", split_axis=0, concat_axis=0, tiled=True),
        ),
        down_map_table=output_down_maps,
        up_map_table=output_up_maps,
    )
    base_terms = block_product(context, output_projection_weight, output_block_scales)
    base_share = lax.psum_scatter(base_terms, "tp", scatter_dimension=1, tiled=True)
    return (base_share + unpack_rows(returned_o)).astype(jnp.bfloat16)


def solution(mesh):
    in_specs = (
        P(("replica", "req"), None),
        P(("replica", "req"), "tp"),
        P(("replica", "req"), "tp"),
        P(("replica", "req"), "tp"),
        P(("replica", "req"), None, "tp"),
        P(("replica", "req"), None, "tp"),
        P(("replica", "req")),
        P(("replica", "req")),
        P("replica"),
        P("tp", None),
        P("tp", None),
        P("req", None, None),
        P("req", None, "tp"),
        P("req", None, "tp"),
        P("req", None, "tp"),
    )
    out_specs = P(("replica", "req"), "tp")
    return jax.shard_map(shards, mesh=mesh, in_specs=in_specs, out_specs=out_specs, check_vma=False)
```

profile of v0, /device:TPU:0, one launch (start us, length us, event | category | flops | bytes accessed | tf_op | source)
XLA Modules:
  0.0 170.2 jit_solution(348360696657896157)
XLA Ops:
  6.5 0.9 select_reduce_fusion.1
  7.8 0.7 sub.25
  8.5 7.3 %all-to-all-start = ((s32[8,1,32]{2,1,0:T(1,128)}), s32[8,1,32]{2,1,0:T(1,128)S(1)}, u32[]{:S(2)}, u32[]{:S(2)}) async-start(s32[8,1,32]{2,1,0:T(1,128)} %sub.25), calls=%async_computation | async-start | bytes 8192 | tf_op jit(solution)/shard_map/all_to_all | solution.py:194
  15.8 1.5 convolution_convert_fusion
  17.3 4.8 %all-to-all-done = s32[8,1,32]{2,1,0:T(1,128)S(1)} async-done(((s32[8,1,32]{2,1,0:T(1,128)}), s32[8,1,32]{2,1,0:T(1,128)S(1)}, u32[]{:S(2)}, u32[]{:S(2)}) %all-to-all-start) | async-done | bytes 1056 | tf_op jit(solution)/shard_map/all_to_all | solution.py:194
  22.2 3.6 %all-to-all-start.1 = ((bf16[8,32,2048]{2,1,0:T(8,128)(2,1)}), bf16[8,32,2048]{2,1,0:T(8,128)(2,1)S(1)}, u32[]{:S(2)}, u32[]{:S(2)}) async-start(bf16[8,32,2048]{2,1,0:T(8,128)(2,1)} %bitcast.1), calls=%async_computation.1 | async-start | bytes 2097152 | tf_op jit(solution)/shard_map/all_to_all | solution.py:193
  25.7 0.5 broadcast.197
  26.2 0.7 reduce.8
  27.0 23.5 %all-to-all-done.1 = bf16[8,32,2048]{2,1,0:T(8,128)(2,1)S(1)} async-done(((bf16[8,32,2048]{2,1,0:T(8,128)(2,1)}), bf16[8,32,2048]{2,1,0:T(8,128)(2,1)S(1)}, u32[]{:S(2)}, u32[]{:S(2)}) %all-to-all-start.1) | async-done | bytes 1048608 | tf_op jit(solution)/shard_map/all_to_all | solution.py:193
  50.5 2.3 %fusion.13 = f32[256,32]{0,1:T(8,128)S(1)} fusion(bf16[256,2048,1]{1,0,2:T(8,128)(2,1)S(1)} %bitcast.92, bf16[16,32,4096]{2,1,0:T(8,128)(2,1)} %param.26, s32[]{:T(128)S(6)} %select_n.47, f32[256,16]{0,1:T(8,128)S(1)} %get-tuple-element.10), kind=kOutput, calls=%fused_computation.20 | convolution fusion | flops 537124864 | bytes 3194884 | tf_op jit(solution)/shard_map/md,ajd->maj/dot_general | solution.py:46
  52.8 3.4 %psum.14 = bf16[256,32]{0,1:T(8,128)(2,1)S(1)} all-reduce(f32[256,32]{0,1:T(8,128)S(1)} %fusion.13), channel_id=1, replica_groups=mesh['replica'=2,'req'=8,'tp'=2] {'tp'}, use_global_device_ids=true, to_apply=%region_4.5 | all-reduce | flops 8192 | bytes 49152 | tf_op jit(solution)/shard_map/psum | solution.py:52
  56.3 0.3 fusion.22
  56.6 0.3 fusion.20
  56.9 1.2 fusion.7
  58.1 3.6 %all-to-all-start.2 = ((bf16[8,32,2048]{2,1,0:T(8,128)(2,1)}), bf16[8,32,2048]{2,1,0:T(8,128)(2,1)S(1)}, u32[]{:S(2)}, u32[]{:S(2)}) async-start(bf16[8,32,2048]{2,1,0:T(8,128)(2,1)} %fusion.7), calls=%async_computation.2 | async-start | bytes 2097152 | tf_op jit(solution)/shard_map/all_to_all | solution.py:69
  62.0 5.3 %copy.62 = bf16[256,8,8,128]{3,2,1,0:T(8,128)(2,1)} copy(bf16[256,8,8,128]{3,1,2,0:T(8,128)(2,1)} %bitcast.85) | data formatting | bytes 8388608
  67.2 9.5 %copy.63 = bf16[128,8,32,128]{3,2,1,0:T(8,128)(2,1)} copy(bf16[128,8,32,128]{3,1,2,0:T(8,128)(2,1)} %bitcast.82) | data formatting | bytes 16777216
  76.8 11.4 %all-to-all-done.2 = bf16[8,32,2048]{2,1,0:T(8,128)(2,1)S(1)} async-done(((bf16[8,32,2048]{2,1,0:T(8,128)(2,1)}), bf16[8,32,2048]{2,1,0:T(8,128)(2,1)S(1)}, u32[]{:S(2)}, u32[]{:S(2)}) %all-to-all-start.2) | async-done | bytes 1048608 | tf_op jit(solution)/shard_map/all_to_all | solution.py:69
  88.2 0.3 fusion.31
  88.9 4.4 %fusion.1 = f32[128,8,1,16]{3,2,1,0:T(1,128)S(1)} fusion(bf16[128,8,128,1]{2,3,1,0:T(2,128)(2,1)S(1)} %reshape.226, bf16[128,16,1024]{2,1,0:T(8,128)(2,1)} %param.19), kind=kOutput, calls=%fused_computation.4 | convolution fusion | flops 4194304 | bytes 4521984 | tf_op jit(solution)/shard_map/rhd,rphd->rhp/dot_general | solution.py:119
  93.4 0.3 copy.39
  94.2 0.5 copy.56
  94.7 4.4 %multiply_reduce_fusion.1 = f32[128,8,128]{2,1,0:T(8,128)S(1)} fusion(f32[128,8,16]{1,2,0:T(8,128)S(1)} %copy.56, bf16[128,16,8,128]{3,2,1,0:T(8,128)(2,1)} %bitcast.81), kind=kLoop, calls=%fused_computation.1 | loop fusion | flops 6160384 | bytes 4784128
  99.6 7.3 %multiply_reduce_fusion = f32[128,32,128]{2,0,1:T(8,128)S(1)} fusion(bf16[8,128,32,128]{3,2,1,0:T(8,128)(2,1)} %bitcast.83, f32[8,32]{1,0:T(8,128)S(1)} %copy-done.8, bf16[128,8,128]{0,2,1:T(8,128)(2,1)S(1)} %add_convert_fusion), kind=kOutput, calls=%fused_computation | convolution fusion | flops 1081606144 | bytes 10748928 | tf_op jit(solution)/shard_map/rkc,kcnd->rknd/dot_general | solution.py:144
  107.0 1.6 copy_bitcast_fusion
  108.6 0.4 convolution_convert_fusion.1
  109.0 18.1 %all_to_all.27 = bf16[8,32,1024]{2,1,0:T(8,128)(2,1)S(1)} all-to-all(bf16[8,32,1024]{2,1,0:T(8,128)(2,1)S(1)} %bitcast.89), channel_id=1, replica_groups=mesh['replica'=2,'req'=8,'tp'=2] {'req'}, dimensions={0} | all-to-all | bytes 1048576 | tf_op jit(solution)/shard_map/all_to_all | solution.py:212
  127.1 0.3 fusion.16
  127.4 3.4 %psum.15 = bf16[256,16]{0,1:T(8,128)(2,1)S(1)} all-reduce(f32[256,16]{0,1:T(8,128)S(1)} %fusion.16), channel_id=1, replica_groups=mesh['replica'=2,'req'=8,'tp'=2] {'tp'}, use_global_device_ids=true, to_apply=%region_10.11 | all-reduce | flops 4096 | bytes 24576 | tf_op jit(solution)/shard_map/psum | solution.py:89
  130.8 0.5 fusion.5
  131.3 29.7 %all_to_all.28 = bf16[8,32,2048]{2,1,0:T(8,128)(2,1)S(1)} all-to-all(bf16[8,32,2048]{2,1,0:T(8,128)(2,1)S(1)} %bitcast.93), channel_id=1, replica_groups=mesh['replica'=2,'req'=8,'tp'=2] {'req'}, dimensions={0} | all-to-all | bytes 2097152 | tf_op jit(solution)/shard_map/all_to_all | solution.py:100
  160.9 2.4 %fusion.6 = bf16[128,2048]{1,0:T(8,128)(2,1)} fusion(f32[128,2048]{1,0:T(8,128)} %reduce-scatter.2.cloned.1.call-done, bf16[256,2048]{1,0:T(8,128)(2,1)S(1)} %bitcast.86, s32[128]{0:T(128)S(1)} %multiply_add_fusion), kind=kOutput, calls=%fused_computation.12 | convolution fusion | flops 134774784 | bytes 2621952 | tf_op jit(solution)/shard_map/dot_general | solution.py:181
  (44 shorter events, 2.0 us)
Async XLA Ops:
  6.5 9.2 %copy-start = (bf16[128,4096]{1,0:T(8,128)(2,1)S(1)}, bf16[128,4096]{1,0:T(8,128)(2,1)}, u32[]{:S(2)}) copy-start(bf16[128,4096]{1,0:T(8,128)(2,1)} %param.15) | copy-start | bytes 3145732
  8.5 13.7 %all-to-all-start = ((s32[8,1,32]{2,1,0:T(1,128)}), s32[8,1,32]{2,1,0:T(1,128)S(1)}, u32[]{:S(2)}, u32[]{:S(2)}) async-start(s32[8,1,32]{2,1,0:T(1,128)} %sub.25), calls=%async_computation | async-start | bytes 8192 | tf_op jit(solution)/shard_map/all_to_all | solution.py:194
  17.3 38.9 %copy-start.5 = (bf16[16,32,1024]{2,1,0:T(8,128)(2,1)S(1)}, bf16[16,32,1024]{2,1,0:T(8,128)(2,1)}, u32[]{:S(2)}) copy-start(bf16[16,32,1024]{2,1,0:T(8,128)(2,1)} %param.27) | copy-start | bytes 3145732
  22.2 28.3 %all-to-all-start.1 = ((bf16[8,32,2048]{2,1,0:T(8,128)(2,1)}), bf16[8,32,2048]{2,1,0:T(8,128)(2,1)S(1)}, u32[]{:S(2)}, u32[]{:S(2)}) async-start(bf16[8,32,2048]{2,1,0:T(8,128)(2,1)} %bitcast.1), calls=%async_computation.1 | async-start | bytes 2097152 | tf_op jit(solution)/shard_map/all_to_all | solution.py:193
  56.9 5.0 %copy-start.3 = (bf16[128,1024]{1,0:T(8,128)(2,1)S(1)}, bf16[128,1024]{1,0:T(8,128)(2,1)}, u32[]{:S(2)}) copy-start(bf16[128,1024]{1,0:T(8,128)(2,1)} %param.17) | copy-start | bytes 786436
  58.1 30.0 %all-to-all-start.2 = ((bf16[8,32,2048]{2,1,0:T(8,128)(2,1)}), bf16[8,32,2048]{2,1,0:T(8,128)(2,1)S(1)}, u32[]{:S(2)}, u32[]{:S(2)}) async-start(bf16[8,32,2048]{2,1,0:T(8,128)(2,1)} %fusion.7), calls=%async_computation.2 | async-start | bytes 2097152 | tf_op jit(solution)/shard_map/all_to_all | solution.py:69
  61.7 99.3 %reduce-scatter.2.cloned.1.call-start = ((), (), s32[]{:S(2)}) async-start(), calls=%async_computation.6 | async-start | bytes 3145728 | tf_op jit(solution)/shard_map/reduce_scatter | solution.py:219
  67.2 9.5 %copy-start.4 = (s32[128]{0:T(128)S(1)}, s32[128]{0:T(128)}, u32[]{:S(2)}) copy-start(s32[128]{0:T(128)} %param.21) | copy-start | bytes 1540
  67.2 21.3 %copy-start.1 = (bf16[128,1024]{1,0:T(8,128)(2,1)S(1)}, bf16[128,1024]{1,0:T(8,128)(2,1)}, u32[]{:S(2)}) copy-start(bf16[128,1024]{1,0:T(8,128)(2,1)} %param.18) | copy-start | bytes 786436
  67.2 21.3 %copy-start.2 = (bf16[128,1024]{1,0:T(8,128)(2,1)S(1)}, bf16[128,1024]{1,0:T(8,128)(2,1)}, u32[]{:S(2)}) copy-start(bf16[128,1024]{1,0:T(8,128)(2,1)} %param.16) | copy-start | bytes 786436
  94.7 4.9 %copy-start.8 = (f32[8,32]{1,0:T(8,128)S(1)}, f32[8,32]{1,0:T(8,128)}, u32[]{:S(2)}) copy-start(f32[8,32]{1,0:T(8,128)} %param.25) | copy-start | bytes 3076
  107.0 20.1 %copy-start.7 = (bf16[16,16,1024]{2,1,0:T(8,128)(2,1)S(1)}, bf16[16,16,1024]{2,1,0:T(8,128)(2,1)}, u32[]{:S(2)}) copy-start(bf16[16,16,1024]{2,1,0:T(8,128)(2,1)} %param.28) | copy-start | bytes 1572868
  107.0 23.9 %copy-start.6 = (bf16[16,16,2048]{2,1,0:T(8,128)(2,1)S(1)}, bf16[16,16,2048]{2,1,0:T(8,128)(2,1)}, u32[]{:S(2)}) copy-start(bf16[16,16,2048]{2,1,0:T(8,128)(2,1)} %param.29) | copy-start | bytes 3145732
Sparse Core Ops, SparseCore 0:
  108.7 8.6 reduce-scatter.1
where the time goes:
time: 171 us; the launch traced here: 170 us
  blocking collectives  54.6 us (32%)
  waiting for transfers between devices  39.7 us (23%)
  matrix products  20.2 us (12%)
  local copies, waits for them, and re-layouts  19.3 us (11%)
  starting transfers between devices  14.6 us (9%)
  between operations  13.7 us (8%)
  other arithmetic  8.08 us (5%)
    all_to_all x1, blocking collectives, o_owner(): lax.all_to_all(output_correction.reshape(owners, pieces, out_width), 'req...  29.7 us
    all_to_all x1, waiting for transfers between devices, shards(): lax.all_to_all(pack_rows(part_rows), 'req', split_axis=0, concat_axis=0,...  23.5 us
    all_to_all x1, blocking collectives, shards(): lax.all_to_all(pack_rows(context), 'req', split_axis=0, concat_axis=0, ti...  18.1 us
    unnamed x23, local copies, waits for them, and re-layouts  15.4 us
    all_to_all x1, waiting for transfers between devices, qv_owner(): lax.all_to_all(adapter_corrections.reshape(owners, pieces, 2 * head_width...  11.4 us
    dot_general x1, matrix products, block_product(): jnp.einsum('rkc,kcnd->rknd', context_blocks, weight_blocks, preferred_ele...  7.32 us
    all_to_all x1, starting transfers between devices, shards(): lax.all_to_all(slots_buf, 'req', split_axis=0, concat_axis=0, tiled=True)  7.28 us
    all_to_all x1, waiting for transfers between devices, shards(): lax.all_to_all(slots_buf, 'req', split_axis=0, concat_axis=0, tiled=True)  4.84 us
  transfers between devices with their start and end apart: 4, of which 3 were waited for; matrix products, arithmetic and copies ran while one was open for 11% of the time, Pallas kernels for 0%

commit v1 on v0

v1 whole, which is shorter than its diff:
```python
import math

import jax
import jax.numpy as jnp
from jax import lax
from jax.experimental import pallas as pl
from jax.experimental.pallas import tpu as pltpu
from jax.sharding import PartitionSpec as P

HEAD_DIM = 128
ADAPTER_RANK = 16
BLOCK = 128
LANES = 128
GROUPS = 2
OUT_CHUNKS = 2
ROW_BLOCK = 16
F32 = jnp.float32
BF16 = jnp.bfloat16
adapter_scale = 2.0


def locate(adapter_of_row, adapter_pool_row, owners, adapter_spread, capacity):
    table_index = jnp.arange(adapter_pool_row.shape[0], dtype=jnp.int32)
    slot_index = jnp.sum(
        jnp.where(adapter_of_row[:, None] == table_index[None, :], adapter_pool_row[None, :], 0),
        axis=1,
    )
    owner = slot_index // adapter_spread
    local_slot = slot_index % adapter_spread
    row_count = adapter_of_row.shape[0]
    row_index = jnp.arange(row_count, dtype=jnp.int32)
    earlier = (owner[:, None] == owner[None, :]) & (row_index[None, :] < row_index[:, None])
    rank_in = jnp.sum(earlier.astype(jnp.int32), axis=1)
    place_index = owner * capacity + rank_in
    slots = jnp.arange(owners * capacity, dtype=jnp.int32)
    placing = (place_index[:, None] == slots[None, :]).astype(BF16)
    placing_t = (place_index[None, :] == slots[:, None]).astype(BF16)
    lanes = jnp.arange(LANES, dtype=jnp.int32)
    chosen = (local_slot[:, None] == lanes[None, :]).astype(BF16)
    return placing, placing_t, chosen


def dot(a, b):
    return jnp.dot(a, b, preferred_element_type=F32)


def dot_t(a, b):
    return lax.dot_general(a, b, (((1,), (1,)), ((), ())), preferred_element_type=F32)


def dot_split(a, b):
    high = a.astype(BF16)
    low = (a - high.astype(F32)).astype(BF16)
    return dot(high, b) + dot(low, b)


def indicator(shape, dim, width):
    wide = lax.broadcasted_iota(jnp.int32, shape, 1 - dim) // width
    narrow = lax.broadcasted_iota(jnp.int32, shape, dim)
    return (wide == narrow).astype(BF16)


def kernel(
    placing, placing_t, chosen, lengths, scales,
    hidden, base_q, key_in, base_v, keys, values, weight, down, up, o_down, o_up,
    out,
    hid_v, bq_v, kin_v, bv_v, keys_v, vals_v, w_v, down_v, up_v, odown_v, oup_v,
    x_send, x_recv, c_send, c_recv, t_send, t_recv, o_send, o_recv,
    sum_send, sum_recv, base_send, base_recv, base_own, q_v, vnew_v, ctx_v, mixed_v, omixed_v,
    local_sem, xs, xr, cs, cr, ts, tr, os_, or_, ps, pr,
):
    n, cap, _ = x_send.shape
    slots = n * cap
    half = hid_v.shape[1]
    rows, width = bq_v.shape
    group = width // GROUPS
    spread2 = mixed_v.shape[1]
    out_half = out.shape[1]
    out_chunk = out_half // OUT_CHUNKS
    me = lax.axis_index("req")
    tp = lax.axis_index("tp")
    other = 1 - tp

    def local(index, src, dst):
        return pltpu.make_async_copy(src, dst, local_sem.at[index])

    feature0 = pl.multiple_of(tp * half, half)
    loads = [
        local(0, hidden.at[:, pl.ds(feature0, half)], hid_v),
        local(1, down.at[:, :, pl.ds(feature0, half)], down_v),
        local(2, up, up_v),
        local(3, base_q, bq_v),
        local(4, base_v, bv_v),
        local(5, key_in, kin_v),
        local(6, keys, keys_v),
        local(7, values, vals_v),
        local(8, o_down, odown_v),
        local(9, weight, w_v),
        local(10, o_up, oup_v),
    ]
    for load in loads:
        load.start()

    barrier = pltpu.get_barrier_semaphore()

    @pl.loop(1, n)
    def _(d):
        pl.semaphore_signal(
            barrier, inc=1, device_id={"req": lax.rem(me + d, n)},
            device_id_type=pl.DeviceIdType.MESH,
        )

    pl.semaphore_signal(
        barrier, inc=1, device_id={"tp": other}, device_id_type=pl.DeviceIdType.MESH
    )

    def copy(send, recv, send_sem, recv_sem, d, slot):
        peer = lax.rem(me + d, n)
        return pltpu.make_async_remote_copy(
            src_ref=send.at[peer],
            dst_ref=recv.at[slot],
            send_sem=send_sem.at[d],
            recv_sem=recv_sem.at[d],
            device_id={"req": peer},
            device_id_type=pl.DeviceIdType.MESH,
        )

    def exchange(send, recv, send_sem, recv_sem):
        @pl.loop(1, n)
        def _(d):
            copy(send, recv, send_sem, recv_sem, d, me).start()

        recv[me] = send[me]

    def arrived(send, recv, send_sem, recv_sem):
        @pl.loop(1, n)
        def _(d):
            copy(send, recv, send_sem, recv_sem, d, lax.rem(me + n - d, n)).wait_recv()

    def sent(send, recv, send_sem, recv_sem):
        @pl.loop(1, n)
        def _(d):
            copy(send, recv, send_sem, recv_sem, d, me).wait_send()

    def sibling(index, src, dst):
        return pltpu.make_async_remote_copy(
            src_ref=src,
            dst_ref=dst,
            send_sem=ps.at[index],
            recv_sem=pr.at[index],
            device_id={"tp": other},
            device_id_type=pl.DeviceIdType.MESH,
        )

    loads[0].wait()
    tile = 512

    @pl.loop(0, half // tile)
    def _(t):
        cols = pl.ds(pl.multiple_of(t * tile, tile), tile)
        packed = dot(placing_t[...], hid_v[:, cols]).astype(BF16)
        x_send[:, :, cols] = packed.reshape(n, cap, tile)

    packed_chosen = dot(placing_t[...], chosen[...]).astype(BF16)
    x_send[:, :, half:] = packed_chosen.reshape(n, cap, LANES)
    pl.semaphore_wait(barrier, n)
    exchange(x_send, x_recv, xs, xr)
    loads[1].wait()
    loads[2].wait()
    arrived(x_send, x_recv, xs, xr)

    picked = x_recv[:, :, half:].reshape(slots, LANES)
    mask = dot(picked, indicator((LANES, spread2), 0, 2 * ADAPTER_RANK))
    shrink = dot_t(
        x_recv[:, :, :half].reshape(slots, half), down_v[...].reshape(spread2, half)
    )
    shrink = shrink * mask
    folded = shrink[:, :LANES]
    for t in range(1, spread2 // LANES):
        folded = folded + shrink[:, t * LANES : (t + 1) * LANES]
    sum_send[0] = folded
    swap = sibling(0, sum_send.at[0], sum_recv.at[0])
    swap.start()
    swap.wait()
    total = (sum_send[0] + sum_recv[0]).astype(BF16).astype(F32)
    mixed_v[...] = (jnp.concatenate([total] * (spread2 // LANES), axis=1) * mask).astype(BF16)

    up_rows = up_v.shape[0] * up_v.shape[1]
    rank_of = lax.broadcasted_iota(jnp.int32, (slots, spread2), 1) % (2 * ADAPTER_RANK)
    is_query = (rank_of < ADAPTER_RANK).astype(BF16)
    mixed_q = mixed_v[...] * is_query
    mixed_val = mixed_v[...] - mixed_q
    for g in range(GROUPS):
        cols = slice(g * group, (g + 1) * group)
        table = up_v[:, :, cols].reshape(up_rows, group)
        for which, mixed in ((0, mixed_q), (1, mixed_val)):
            corr = (adapter_scale * dot(mixed, table)).astype(BF16)
            c = 2 * g + which
            c_send[c] = corr.reshape(n, cap, group)
            exchange(c_send.at[c], c_recv.at[c], cs.at[c], cr.at[c])

    for index in range(3, 9):
        loads[index].wait()
    inverse_root = 1.0 / math.sqrt(HEAD_DIM)
    cache = keys_v.shape[1]
    gather = indicator((group, LANES), 1, HEAD_DIM)
    spreadm = indicator((LANES, group), 0, HEAD_DIM)
    position = lax.broadcasted_iota(jnp.int32, (ROW_BLOCK, cache, LANES), 1)
    for g in range(GROUPS):
        cols = slice(g * group, (g + 1) * group)
        for which, base, dest in ((0, bq_v, q_v), (1, bv_v, vnew_v)):
            c = 2 * g + which
            arrived(c_send.at[c], c_recv.at[c], cs.at[c], cr.at[c])
            corr = dot(placing[...], c_recv[c].reshape(slots, group))
            dest[:, cols] = (base[:, cols].astype(F32) + corr).astype(BF16)

        @pl.loop(0, rows // ROW_BLOCK)
        def _(i):
            block = pl.ds(pl.multiple_of(i * ROW_BLOCK, ROW_BLOCK), ROW_BLOCK)
            q = q_v[block, cols].astype(F32)
            product = keys_v[block, :, cols].astype(F32) * q[:, None, :]
            score = dot_split(product.reshape(ROW_BLOCK * cache, group), gather) * inverse_root
            score = score.reshape(ROW_BLOCK, cache, LANES)
            own = dot_split(q * kin_v[block, cols].astype(F32), gather) * inverse_root
            usable = position < lengths[block, :][:, None, :]
            score = jnp.where(usable, score, -jnp.inf)
            highest = jnp.maximum(jnp.max(score, axis=1), own)
            e = jnp.exp(score - highest[:, None, :])
            own_e = jnp.exp(own - highest)
            denominator = jnp.sum(e, axis=1) + own_e
            w = (e / denominator[:, None, :]).reshape(ROW_BLOCK * cache, LANES).astype(BF16)
            own_w = (own_e / denominator).astype(BF16)
            wide = dot(w, spreadm).reshape(ROW_BLOCK, cache, group)
            context = jnp.sum(wide * vals_v[block, :, cols].astype(F32), axis=1)
            context = context + dot(own_w, spreadm) * vnew_v[block, cols].astype(F32)
            ctx_v[block, cols] = context.astype(BF16)

        packed = dot(placing_t[...], ctx_v[:, cols]).astype(BF16)
        t_send[g] = packed.reshape(n, cap, group)
        exchange(t_send.at[g], t_recv.at[g], ts.at[g], tr.at[g])

    loads[9].wait()
    loads[10].wait()

    def project(column):
        total = None
        for k in range(width // BLOCK):
            part = dot(ctx_v[:, k * BLOCK : (k + 1) * BLOCK], w_v[k * BLOCK : (k + 1) * BLOCK, column])
            part = part * scales[k : k + 1, column]
            total = part if total is None else total + part
        return total

    @pl.loop(0, out_half // tile)
    def _(t):
        column = pl.ds(pl.multiple_of(other * out_half + t * tile, tile), tile)
        base_send[:, pl.ds(pl.multiple_of(t * tile, tile), tile)] = project(column)

    base_swap = sibling(2, base_send, base_recv)

    omask = dot(picked, indicator((LANES, omixed_v.shape[1]), 0, ADAPTER_RANK))
    orows = odown_v.shape[0] * odown_v.shape[1]
    oshrink = None
    for g in range(GROUPS):
        arrived(t_send.at[g], t_recv.at[g], ts.at[g], tr.at[g])
        part = dot_t(
            t_recv[g].reshape(slots, group),
            odown_v[:, :, g * group : (g + 1) * group].reshape(orows, group),
        )
        oshrink = part if oshrink is None else oshrink + part
    oshrink = oshrink * omask
    ofolded = oshrink[:, :LANES]
    for t in range(1, orows // LANES):
        ofolded = ofolded + oshrink[:, t * LANES : (t + 1) * LANES]
    sum_send[1] = ofolded
    oswap = sibling(1, sum_send.at[1], sum_recv.at[1])
    oswap.start()
    oswap.wait()
    base_swap.start()
    ototal = (sum_send[1] + sum_recv[1]).astype(BF16).astype(F32)
    omixed_v[...] = (jnp.concatenate([ototal] * (orows // LANES), axis=1) * omask).astype(BF16)
    for c in range(OUT_CHUNKS):
        table = oup_v[:, :, c * out_chunk : (c + 1) * out_chunk].reshape(orows, out_chunk)
        corr = (adapter_scale * dot(omixed_v[...], table)).astype(BF16)
        o_send[c] = corr.reshape(n, cap, out_chunk)
        exchange(o_send.at[c], o_recv.at[c], os_.at[c], or_.at[c])

    @pl.loop(0, out_half // tile)
    def _(t):
        column = pl.ds(pl.multiple_of(tp * out_half + t * tile, tile), tile)
        base_own[:, pl.ds(pl.multiple_of(t * tile, tile), tile)] = project(column)

    base_swap.wait()
    for c in range(OUT_CHUNKS):
        cols = slice(c * out_chunk, (c + 1) * out_chunk)
        arrived(o_send.at[c], o_recv.at[c], os_.at[c], or_.at[c])
        corr = dot(placing[...], o_recv[c].reshape(slots, out_chunk))
        out[:, cols] = (base_own[:, cols] + base_recv[:, cols] + corr).astype(BF16)

    sent(x_send, x_recv, xs, xr)
    for c in range(2 * GROUPS):
        sent(c_send.at[c], c_recv.at[c], cs.at[c], cr.at[c])
    for g in range(GROUPS):
        sent(t_send.at[g], t_recv.at[g], ts.at[g], tr.at[g])
    for c in range(OUT_CHUNKS):
        sent(o_send.at[c], o_recv.at[c], os_.at[c], or_.at[c])


def shards(
    normed_hidden_rows,
    base_query_rows,
    incoming_key,
    base_value_rows,
    stored_keys,
    stored_values,
    cache_fill_length,
    adapter_of_row,
    adapter_pool_row,
    output_projection_weight,
    output_block_scales,
    query_value_down_maps,
    query_value_up_maps,
    output_down_maps,
    output_up_maps,
):
    n = lax.axis_size("req")
    spread = query_value_down_maps.shape[0]
    rows, model_width = normed_hidden_rows.shape
    width = base_query_rows.shape[1]
    cap = max(16, 2 * ((rows + n - 1) // n))
    slots = n * cap
    half = model_width // lax.axis_size("tp")
    out_half = output_up_maps.shape[2]
    group = width // GROUPS
    out_chunk = out_half // OUT_CHUNKS
    placing, placing_t, chosen = locate(adapter_of_row, adapter_pool_row, n, spread, cap)
    lengths = jnp.broadcast_to(cache_fill_length[:, None], (rows, LANES))
    scales = jnp.repeat(output_block_scales, BLOCK, axis=1)
    vmem = pl.BlockSpec(memory_space=pltpu.VMEM)
    hbm = pl.BlockSpec(memory_space=pl.ANY)

    def like(x):
        return pltpu.VMEM(x.shape, x.dtype)

    dma = pltpu.SemaphoreType.DMA
    return pl.pallas_call(
        kernel,
        out_shape=jax.ShapeDtypeStruct((rows, out_half), BF16),
        in_specs=[vmem] * 5 + [hbm] * 11,
        out_specs=vmem,
        scratch_shapes=[
            pltpu.VMEM((rows, half), BF16),
            like(base_query_rows),
            like(incoming_key),
            like(base_value_rows),
            like(stored_keys),
            like(stored_values),
            like(output_projection_weight),
            pltpu.VMEM((spread, query_value_down_maps.shape[1], half), BF16),
            like(query_value_up_maps),
            like(output_down_maps),
            like(output_up_maps),
            pltpu.VMEM((n, cap, half + LANES), BF16),
            pltpu.VMEM((n, cap, half + LANES), BF16),
            pltpu.VMEM((2 * GROUPS, n, cap, group), BF16),
            pltpu.VMEM((2 * GROUPS, n, cap, group), BF16),
            pltpu.VMEM((GROUPS, n, cap, group), BF16),
            pltpu.VMEM((GROUPS, n, cap, group), BF16),
            pltpu.VMEM((OUT_CHUNKS, n, cap, out_chunk), BF16),
            pltpu.VMEM((OUT_CHUNKS, n, cap, out_chunk), BF16),
            pltpu.VMEM((2, slots, LANES), F32),
            pltpu.VMEM((2, slots, LANES), F32),
            pltpu.VMEM((rows, out_half), F32),
            pltpu.VMEM((rows, out_half), F32),
            pltpu.VMEM((rows, out_half), F32),
            pltpu.VMEM((rows, width), BF16),
            pltpu.VMEM((rows, width), BF16),
            pltpu.VMEM((rows, width), BF16),
            pltpu.VMEM((slots, spread * 2 * ADAPTER_RANK), BF16),
            pltpu.VMEM((slots, spread * ADAPTER_RANK), BF16),
            dma((11,)),
            dma((n,)),
            dma((n,)),
            dma((2 * GROUPS, n)),
            dma((2 * GROUPS, n)),
            dma((GROUPS, n)),
            dma((GROUPS, n)),
            dma((OUT_CHUNKS, n)),
            dma((OUT_CHUNKS, n)),
            dma((3,)),
            dma((3,)),
        ],
        compiler_params=pltpu.CompilerParams(
            collective_id=0, has_side_effects=True, vmem_limit_bytes=58 * 1024 * 1024
        ),
    )(
        placing, placing_t, chosen, lengths, scales,
        normed_hidden_rows, base_query_rows, incoming_key, base_value_rows,
        stored_keys, stored_values, output_projection_weight,
        query_value_down_maps, query_value_up_maps, output_down_maps, output_up_maps,
    )


def solution(mesh):
    in_specs = (
        P(("replica", "req"), None),
        P(("replica", "req"), "tp"),
        P(("replica", "req"), "tp"),
        P(("replica", "req"), "tp"),
        P(("replica", "req"), None, "tp"),
        P(("replica", "req"), None, "tp"),
        P(("replica", "req")),
        P(("replica", "req")),
        P("replica"),
        P("tp", None),
        P("tp", None),
        P("req", None, None),
        P("req", None, "tp"),
        P("req", None, "tp"),
        P("req", None, "tp"),
    )
    out_specs = P(("replica", "req"), "tp")
    return jax.shard_map(shards, mesh=mesh, in_specs=in_specs, out_specs=out_specs, check_vma=False)
```

time: 171 us -> 106 us (0.62)
  Pallas kernels: 0 us -> 96.6 us
  blocking collectives: 54.6 us -> 0 us
  waiting for transfers between devices: 39.7 us -> 0 us
  matrix products: 20.2 us -> 0 us
  starting transfers between devices: 14.6 us -> 0 us
  local copies, waits for them, and re-layouts: 19.3 us -> 4.76 us
  between operations: 13.7 us -> 0.04 us
  other arithmetic: 8.08 us -> 3.06 us
    pallas_call x0 -> x1, Pallas kernels: none -> 96.6 us  [shards(): pl.pallas_call(kernel, out_shape=jax.ShapeDtypeStruct((rows, out_half), B...]
    all_to_all x2 -> x0, blocking collectives: 47.8 us -> none  [the longest x1 29.7 us: o_owner(): lax.all_to_all(output_correction.reshape(owners, pieces, out_width), 'req...]
    all_to_all x3 -> x0, waiting for transfers between devices: 39.7 us -> none  [the longest x1 23.5 us: shards(): lax.all_to_all(pack_rows(part_rows), 'req', split_axis=0, concat_axis=0,...]
    dot_general x11 -> x0, matrix products: 20.2 us -> none  [the longest x1 7.32 us: block_product(): jnp.einsum('rkc,kcnd->rknd', context_blocks, weight_blocks, preferred_ele...]
    all_to_all x3 -> x0, starting transfers between devices: 14.4 us -> none  [the longest x1 7.28 us: shards(): lax.all_to_all(slots_buf, 'req', split_axis=0, concat_axis=0, tiled=True)]
    unnamed x23 -> x2, local copies, waits for them, and re-layouts: 15.4 us -> 2.65 us
    psum x2 -> x0, blocking collectives: 6.78 us -> none  [the longest x1 3.41 us: qv_owner(): rank_projection = lax.psum(rank_projection, 'tp')]
    unnamed x3 -> x0, other arithmetic: 4.65 us -> none
  transfers between devices with their start and end apart: 4 -> 0, of which waited for: 3 -> 0; matrix products, arithmetic and copies ran while one was open for 11% -> 0% of each run, Pallas kernels for 0% -> 0%
where the time goes in v1:
time: 106 us; the launch traced here: 104 us
  Pallas kernels  96.6 us (91%)
  local copies, waits for them, and re-layouts  4.76 us (4%)
  other arithmetic  3.06 us (3%)
    pallas_call x1, Pallas kernels, shards(): pl.pallas_call(kernel, out_shape=jax.ShapeDtypeStruct((rows, out_half), B...  96.6 us
    unnamed x2, local copies, waits for them, and re-layouts  2.65 us

profile of v1, /device:TPU:0, one launch (start us, length us, event | category | flops | bytes accessed | tf_op | source)
XLA Modules:
  0.0 104.5 jit_solution(13318611453360269475)
XLA Ops:
  0.0 0.8 select_reduce_fusion
  0.9 0.2 convert_reduce_fusion
  1.1 0.8 copy.17
  1.8 0.7 fusion.3.chosen
  2.5 0.6 fusion.1.placing_t
  3.1 0.7 fusion.placing
  3.9 1.4 %broadcast_in_dim.18.lengths = s32[128,128]{1,0:T(8,128)} broadcast(s32[128]{0:T(128)} %param.21), dimensions={0} | broadcast | bytes 66048 | tf_op jit(solution)/shard_map/broadcast_in_dim | solution.py:336
  5.2 0.8 broadcast_bitcast_fusion.scales
  6.0 96.6 %shard_map.145 = bf16[128,2048]{1,0:T(8,128)(2,1)} custom-call(bf16[128,256]{1,0:T(8,128)(2,1)} %fusion.placing, bf16[256,128]{1,0:T(8,128)(2,1)} %fusion.1.placing_t, bf16[128,128]{1,0:T(8,128)(2,1)} %fusion.3.chosen, s32[128,128]{1,0:T(8,128)} %broadcast_in_dim.18.lengths, f32[8,4096]{1,0:T(8,128)} %broadcast_bitcast_fusion.scales, ...), custom_call_target="tpu_custom_call" | custom-call | tf_op jit(solution)/shard_map/pallas_call | solution.py:345
  102.6 1.9 %copy.19 = bf16[128,2048]{1,0:T(8,128)(2,1)} copy(bf16[128,2048]{1,0:T(8,128)(2,1)} %shard_map.145) | data formatting | bytes 1048576
  (2 shorter events, 0.0 us)

commit v2 on v1

v2 whole, which is shorter than its diff:
```python
import math

import jax
import jax.numpy as jnp
from jax import lax
from jax.experimental import pallas as pl
from jax.experimental.pallas import tpu as pltpu
from jax.sharding import PartitionSpec as P

HEAD_DIM = 128
ADAPTER_RANK = 16
BLOCK = 128
LANES = 128
GROUPS = 2
OUT_CHUNKS = 2
ROW_BLOCK = 32
SUB = 16
F32 = jnp.float32
BF16 = jnp.bfloat16
adapter_scale = 2.0


def dot(a, b):
    return jnp.dot(a, b, preferred_element_type=F32)


def dot_t(a, b):
    return lax.dot_general(a, b, (((1,), (1,)), ((), ())), preferred_element_type=F32)


def dot_split(a, b):
    high = a.astype(BF16)
    low = (a - high.astype(F32)).astype(BF16)
    return dot(high, b) + dot(low, b)


def indicator(shape, dim, width):
    wide = lax.broadcasted_iota(jnp.int32, shape, 1 - dim) // width
    narrow = lax.broadcasted_iota(jnp.int32, shape, dim)
    return (wide == narrow).astype(BF16)


def column(row):
    return jnp.transpose(jnp.broadcast_to(row, (LANES, LANES)))


def kernel(
    adapter_of_row, adapter_pool_row, fill, scales,
    hidden, base_q, key_in, base_v, keys, values, weight, down, up, o_down, o_up,
    out,
    hid_v, bq_v, kin_v, bv_v, keys_v, vals_v, w_v, down_v, up_v, odown_v, oup_v,
    placing, placing_t, lengths, wide_scales,
    x_send, x_recv, c_send, c_recv, t_send, t_recv, o_send, o_recv,
    sum_send, sum_recv, base_send, base_recv, base_own, q_v, vnew_v, ctx_v, mixed_v, omixed_v,
    local_sem, xs, xr, cs, cr, ts, tr, os_, or_, ps, pr,
):
    halves, n, sub, _ = x_send.shape
    part = n * sub
    half = hid_v.shape[1]
    rows, width = bq_v.shape
    group = width // GROUPS
    spread = odown_v.shape[0]
    spread2 = mixed_v.shape[2]
    orows = omixed_v.shape[2]
    out_half = out.shape[1]
    out_chunk = out_half // OUT_CHUNKS
    me = lax.axis_index("req")
    tp = lax.axis_index("tp")
    other = 1 - tp

    def local(index, src, dst):
        return pltpu.make_async_copy(src, dst, local_sem.at[index])

    feature0 = pl.multiple_of(tp * half, half)
    loads = [
        local(0, hidden.at[:, pl.ds(feature0, half)], hid_v),
        local(1, down.at[:, :, pl.ds(feature0, half)], down_v),
        local(2, up, up_v),
        local(3, base_q, bq_v),
        local(4, base_v, bv_v),
        local(5, key_in, kin_v),
        local(6, keys, keys_v),
        local(7, values, vals_v),
        local(8, o_down, odown_v),
        local(9, weight, w_v),
        local(10, o_up, oup_v),
    ]
    loads[0].start()

    barrier = pltpu.get_barrier_semaphore()

    @pl.loop(1, n)
    def _(d):
        pl.semaphore_signal(
            barrier, inc=1, device_id={"req": lax.rem(me + d, n)},
            device_id_type=pl.DeviceIdType.MESH,
        )

    pl.semaphore_signal(
        barrier, inc=1, device_id={"tp": other}, device_id_type=pl.DeviceIdType.MESH
    )

    def copy(send, recv, send_sem, recv_sem, d, slot):
        peer = lax.rem(me + d, n)
        return pltpu.make_async_remote_copy(
            src_ref=send.at[peer],
            dst_ref=recv.at[slot],
            send_sem=send_sem.at[d],
            recv_sem=recv_sem.at[d],
            device_id={"req": peer},
            device_id_type=pl.DeviceIdType.MESH,
        )

    def exchange(send, recv, send_sem, recv_sem):
        @pl.loop(1, n)
        def _(d):
            copy(send, recv, send_sem, recv_sem, d, me).start()

        recv[me] = send[me]

    def arrived(send, recv, send_sem, recv_sem):
        @pl.loop(1, n)
        def _(d):
            copy(send, recv, send_sem, recv_sem, d, lax.rem(me + n - d, n)).wait_recv()

    def sent(send, recv, send_sem, recv_sem):
        @pl.loop(1, n)
        def _(d):
            copy(send, recv, send_sem, recv_sem, d, me).wait_send()

    def hidden_move(h):
        return x_send.at[h], x_recv.at[h], xs.at[h], xr.at[h]

    def corr_move(g, h):
        i = g * halves + h
        return c_send.at[i], c_recv.at[i], cs.at[i], cr.at[i]

    def context_move(g, h):
        i = g * halves + h
        return t_send.at[i], t_recv.at[i], ts.at[i], tr.at[i]

    def out_move(h, c):
        i = h * OUT_CHUNKS + c
        return o_send.at[i], o_recv.at[i], os_.at[i], or_.at[i]

    def sibling(index, src, dst):
        return pltpu.make_async_remote_copy(
            src_ref=src,
            dst_ref=dst,
            send_sem=ps.at[index],
            recv_sem=pr.at[index],
            device_id={"tp": other},
            device_id_type=pl.DeviceIdType.MESH,
        )

    pool = adapter_pool_row.shape[1]
    named = lax.broadcasted_iota(jnp.int32, (pool, rows), 0) == adapter_of_row[...]
    named = named.astype(F32).astype(BF16)
    stored = jnp.broadcast_to(adapter_pool_row[...], (16, pool))
    owner = dot((stored // spread).astype(F32).astype(BF16), named)[:1]
    local_slot = dot((stored % spread).astype(F32).astype(BF16), named)[:1]
    lower = lax.broadcasted_iota(jnp.int32, (rows, rows), 0) < lax.broadcasted_iota(
        jnp.int32, (rows, rows), 1
    )
    earlier = (column(owner) == owner) & lower
    rank = jnp.sum(earlier.astype(F32), axis=0, keepdims=True).astype(jnp.int32)
    place = (rank // sub) * part + owner.astype(jnp.int32) * sub + rank % sub
    slots = halves * part
    placing_t[...] = (
        (lax.broadcasted_iota(jnp.int32, (slots, rows), 0) == place).astype(F32).astype(BF16)
    )
    place_c = column(place.astype(F32)).astype(jnp.int32)
    lane = lax.broadcasted_iota(jnp.int32, (rows, LANES), 1)
    for t in range(slots // LANES):
        here = (lane + t * LANES == place_c).astype(F32).astype(BF16)
        placing[:, t * LANES : (t + 1) * LANES] = here
    chosen = (lane == column(local_slot).astype(jnp.int32)).astype(F32).astype(BF16)
    lengths[...] = column(fill[...].astype(F32)).astype(jnp.int32)

    loads[0].wait()
    for load in loads[1:4]:
        load.start()
    tile = 512
    for h in range(halves):
        pick = slice(h * part, (h + 1) * part)

        @pl.loop(0, half // tile)
        def _(t):
            cols = pl.ds(pl.multiple_of(t * tile, tile), tile)
            packed = dot(placing_t[pick], hid_v[:, cols]).astype(BF16)
            x_send[h, :, :, cols] = packed.reshape(n, sub, tile)

        packed_chosen = dot(placing_t[pick], chosen).astype(BF16)
        x_send[h, :, :, half:] = packed_chosen.reshape(n, sub, LANES)
        if h == 0:
            pl.semaphore_wait(barrier, n)
        exchange(*hidden_move(h))
    for load in loads[4:]:
        load.start()

    high = scales[...].astype(BF16)
    rest = scales[...] - high.astype(F32)
    middle = rest.astype(BF16)
    low = (rest - middle.astype(F32)).astype(BF16)
    blocks = scales.shape[1]
    block_of = lax.broadcasted_iota(jnp.int32, (blocks, tile), 0)
    block_at = lax.broadcasted_iota(jnp.int32, (blocks, tile), 1) // BLOCK
    for t in range(wide_scales.shape[1] // tile):
        chosen_block = (block_of == block_at + t * (tile // BLOCK)).astype(F32).astype(BF16)
        wide_scales[:, t * tile : (t + 1) * tile] = (
            dot(high, chosen_block) + dot(middle, chosen_block) + dot(low, chosen_block)
        )

    loads[1].wait()
    loads[2].wait()

    def sum_cores(index, shrink, mask):
        pieces = shrink.shape[1] // LANES
        shrink = shrink * mask
        folded = shrink[:, :LANES]
        for t in range(1, pieces):
            folded = folded + shrink[:, t * LANES : (t + 1) * LANES]
        sum_send[index] = folded
        swap = sibling(index, sum_send.at[index], sum_recv.at[index])
        swap.start()
        swap.wait()
        total = (sum_send[index] + sum_recv[index]).astype(BF16).astype(F32)
        return (jnp.concatenate([total] * pieces, axis=1) * mask).astype(BF16)

    def picked(h):
        return x_recv[h, :, :, half:].reshape(part, LANES)

    rank_of = lax.broadcasted_iota(jnp.int32, (part, spread2), 1) % (2 * ADAPTER_RANK)
    is_query = (rank_of < ADAPTER_RANK).astype(F32).astype(BF16)

    def correct(g, h):
        mixed = mixed_v[h]
        mixed_q = mixed * is_query
        table = up_v[:, :, g * group : (g + 1) * group].reshape(spread2, group)
        i = g * halves + h
        corr = (adapter_scale * dot(mixed_q, table)).astype(BF16)
        c_send[i, :, :, :group] = corr.reshape(n, sub, group)
        corr = (adapter_scale * dot(mixed - mixed_q, table)).astype(BF16)
        c_send[i, :, :, group:] = corr.reshape(n, sub, group)
        exchange(*corr_move(g, h))

    for h in range(halves):
        arrived(*hidden_move(h))
        mask = dot(picked(h), indicator((LANES, spread2), 0, 2 * ADAPTER_RANK))
        shrink = dot_t(
            x_recv[h, :, :, :half].reshape(part, half), down_v[...].reshape(spread2, half)
        )
        mixed_v[h] = sum_cores(h, shrink, mask)
        correct(0, h)
    for g in range(1, GROUPS):
        for h in range(halves):
            correct(g, h)

    for index in range(3, 9):
        loads[index].wait()
    inverse_root = 1.0 / math.sqrt(HEAD_DIM)
    cache = keys_v.shape[1]
    gather = indicator((group, LANES), 1, HEAD_DIM)
    spreadm = indicator((LANES, group), 0, HEAD_DIM)
    position = lax.broadcasted_iota(jnp.int32, (ROW_BLOCK, cache, LANES), 1)
    for g in range(GROUPS):
        cols = slice(g * group, (g + 1) * group)
        corr = None
        for h in range(halves):
            arrived(*corr_move(g, h))
            term = dot(
                placing[:, h * part : (h + 1) * part],
                c_recv[g * halves + h].reshape(part, 2 * group),
            )
            corr = term if corr is None else corr + term
        q_v[:, cols] = (bq_v[:, cols].astype(F32) + corr[:, :group]).astype(BF16)
        vnew_v[:, cols] = (bv_v[:, cols].astype(F32) + corr[:, group:]).astype(BF16)

        @pl.loop(0, rows // ROW_BLOCK)
        def _(i):
            block = pl.ds(pl.multiple_of(i * ROW_BLOCK, ROW_BLOCK), ROW_BLOCK)
            q = q_v[block, cols].astype(F32)
            product = keys_v[block, :, cols].astype(F32) * q[:, None, :]
            score = dot_split(product.reshape(ROW_BLOCK * cache, group), gather) * inverse_root
            score = score.reshape(ROW_BLOCK, cache, LANES)
            own = dot_split(q * kin_v[block, cols].astype(F32), gather) * inverse_root
            usable = position < lengths[block, :][:, None, :]
            score = jnp.where(usable, score, -jnp.inf)
            highest = jnp.maximum(jnp.max(score, axis=1), own)
            e = jnp.exp(score - highest[:, None, :])
            own_e = jnp.exp(own - highest)
            denominator = jnp.sum(e, axis=1) + own_e
            w = (e / denominator[:, None, :]).reshape(ROW_BLOCK * cache, LANES).astype(BF16)
            own_w = (own_e / denominator).astype(BF16)
            wide = dot(w, spreadm).reshape(ROW_BLOCK, cache, group)
            context = jnp.sum(wide * vals_v[block, :, cols].astype(F32), axis=1)
            context = context + dot(own_w, spreadm) * vnew_v[block, cols].astype(F32)
            ctx_v[block, cols] = context.astype(BF16)

        for h in range(halves):
            packed = dot(placing_t[h * part : (h + 1) * part], ctx_v[:, cols]).astype(BF16)
            t_send[g * halves + h] = packed.reshape(n, sub, group)
            exchange(*context_move(g, h))

    loads[9].wait()
    loads[10].wait()

    def project(columns):
        total = None
        for k in range(width // BLOCK):
            span = slice(k * BLOCK, (k + 1) * BLOCK)
            term = dot(ctx_v[:, span], w_v[span, columns]) * wide_scales[k : k + 1, columns]
            total = term if total is None else total + term
        return total

    @pl.loop(0, out_half // tile)
    def _(t):
        columns = pl.ds(pl.multiple_of(other * out_half + t * tile, tile), tile)
        base_send[:, pl.ds(pl.multiple_of(t * tile, tile), tile)] = project(columns)

    base_swap = sibling(2 * halves, base_send, base_recv)

    for h in range(halves):
        omask = dot(picked(h), indicator((LANES, orows), 0, ADAPTER_RANK))
        oshrink = None
        for g in range(GROUPS):
            arrived(*context_move(g, h))
            term = dot_t(
                t_recv[g * halves + h].reshape(part, group),
                odown_v[:, :, g * group : (g + 1) * group].reshape(orows, group),
            )
            oshrink = term if oshrink is None else oshrink + term
        omixed_v[h] = sum_cores(halves + h, oshrink, omask)
        for c in range(OUT_CHUNKS):
            table = oup_v[:, :, c * out_chunk : (c + 1) * out_chunk].reshape(orows, out_chunk)
            corr = (adapter_scale * dot(omixed_v[h], table)).astype(BF16)
            o_send[h * OUT_CHUNKS + c] = corr.reshape(n, sub, out_chunk)
            exchange(*out_move(h, c))
    base_swap.start()

    @pl.loop(0, out_half // tile)
    def _(t):
        columns = pl.ds(pl.multiple_of(tp * out_half + t * tile, tile), tile)
        base_own[:, pl.ds(pl.multiple_of(t * tile, tile), tile)] = project(columns)

    base_swap.wait()
    for h in range(halves):
        for c in range(OUT_CHUNKS):
            cols = slice(c * out_chunk, (c + 1) * out_chunk)
            arrived(*out_move(h, c))
            total = base_own[:, cols] + dot(
                placing[:, h * part : (h + 1) * part],
                o_recv[h * OUT_CHUNKS + c].reshape(part, out_chunk),
            )
            if h == 0:
                total = total + base_recv[:, cols]
            if h == halves - 1:
                out[:, cols] = total.astype(BF16)
            else:
                base_own[:, cols] = total

    for h in range(halves):
        sent(*hidden_move(h))
        for g in range(GROUPS):
            sent(*corr_move(g, h))
            sent(*context_move(g, h))
        for c in range(OUT_CHUNKS):
            sent(*out_move(h, c))


def shards(
    normed_hidden_rows,
    base_query_rows,
    incoming_key,
    base_value_rows,
    stored_keys,
    stored_values,
    cache_fill_length,
    adapter_of_row,
    adapter_pool_row,
    output_projection_weight,
    output_block_scales,
    query_value_down_maps,
    query_value_up_maps,
    output_down_maps,
    output_up_maps,
):
    n = lax.axis_size("req")
    spread = query_value_down_maps.shape[0]
    rows, model_width = normed_hidden_rows.shape
    width = base_query_rows.shape[1]
    halves = (2 * ((rows + n - 1) // n) + SUB - 1) // SUB
    part = n * SUB
    slots = halves * part
    half = model_width // lax.axis_size("tp")
    out_half = output_up_maps.shape[2]
    group = width // GROUPS
    out_chunk = out_half // OUT_CHUNKS
    vmem = pl.BlockSpec(memory_space=pltpu.VMEM)
    hbm = pl.BlockSpec(memory_space=pl.ANY)

    def like(x):
        return pltpu.VMEM(x.shape, x.dtype)

    dma = pltpu.SemaphoreType.DMA
    return pl.pallas_call(
        kernel,
        out_shape=jax.ShapeDtypeStruct((rows, out_half), BF16),
        in_specs=[vmem] * 4 + [hbm] * 11,
        out_specs=vmem,
        scratch_shapes=[
            pltpu.VMEM((rows, half), BF16),
            like(base_query_rows),
            like(incoming_key),
            like(base_value_rows),
            like(stored_keys),
            like(stored_values),
            like(output_projection_weight),
            pltpu.VMEM((spread, query_value_down_maps.shape[1], half), BF16),
            like(query_value_up_maps),
            like(output_down_maps),
            like(output_up_maps),
            pltpu.VMEM((rows, slots), BF16),
            pltpu.VMEM((slots, rows), BF16),
            pltpu.VMEM((rows, LANES), jnp.int32),
            pltpu.VMEM((output_block_scales.shape[0], model_width), F32),
            pltpu.VMEM((halves, n, SUB, half + LANES), BF16),
            pltpu.VMEM((halves, n, SUB, half + LANES), BF16),
            pltpu.VMEM((GROUPS * halves, n, SUB, 2 * group), BF16),
            pltpu.VMEM((GROUPS * halves, n, SUB, 2 * group), BF16),
            pltpu.VMEM((GROUPS * halves, n, SUB, group), BF16),
            pltpu.VMEM((GROUPS * halves, n, SUB, group), BF16),
            pltpu.VMEM((OUT_CHUNKS * halves, n, SUB, out_chunk), BF16),
            pltpu.VMEM((OUT_CHUNKS * halves, n, SUB, out_chunk), BF16),
            pltpu.VMEM((2 * halves, part, LANES), F32),
            pltpu.VMEM((2 * halves, part, LANES), F32),
            pltpu.VMEM((rows, out_half), F32),
            pltpu.VMEM((rows, out_half), F32),
            pltpu.VMEM((rows, out_half), F32),
            pltpu.VMEM((rows, width), BF16),
            pltpu.VMEM((rows, width), BF16),
            pltpu.VMEM((rows, width), BF16),
            pltpu.VMEM((halves, part, spread * 2 * ADAPTER_RANK), BF16),
            pltpu.VMEM((halves, part, spread * ADAPTER_RANK), BF16),
            dma((11,)),
            dma((halves, n)),
            dma((halves, n)),
            dma((GROUPS * halves, n)),
            dma((GROUPS * halves, n)),
            dma((GROUPS * halves, n)),
            dma((GROUPS * halves, n)),
            dma((OUT_CHUNKS * halves, n)),
            dma((OUT_CHUNKS * halves, n)),
            dma((2 * halves + 1,)),
            dma((2 * halves + 1,)),
        ],
        compiler_params=pltpu.CompilerParams(
            collective_id=0, has_side_effects=True, vmem_limit_bytes=58 * 1024 * 1024
        ),
    )(
        adapter_of_row[None, :], adapter_pool_row[None, :], cache_fill_length[None, :],
        output_block_scales, normed_hidden_rows, base_query_rows, incoming_key, base_value_rows,
        stored_keys, stored_values, output_projection_weight,
        query_value_down_maps, query_value_up_maps, output_down_maps, output_up_maps,
    )


def solution(mesh):
    in_specs = (
        P(("replica", "req"), None),
        P(("replica", "req"), "tp"),
        P(("replica", "req"), "tp"),
        P(("replica", "req"), "tp"),
        P(("replica", "req"), None, "tp"),
        P(("replica", "req"), None, "tp"),
        P(("replica", "req")),
        P(("replica", "req")),
        P("replica"),
        P("tp", None),
        P("tp", None),
        P("req", None, None),
        P("req", None, "tp"),
        P("req", None, "tp"),
        P("req", None, "tp"),
    )
    out_specs = P(("replica", "req"), "tp")
    return jax.shard_map(shards, mesh=mesh, in_specs=in_specs, out_specs=out_specs, check_vma=False)
```

time: 106 us -> 97.6 us (0.921); the launches traced: 104 us -> 97.3 us
  other arithmetic: 3.06 us -> 0 us
  local copies, waits for them, and re-layouts: 4.76 us -> 1.88 us
  Pallas kernels: 96.6 us -> 95.5 us
    convert_element_type x3 -> x0, other arithmetic: 2.03 us -> none  [the longest x1 0.71 us: locate(): placing = (place_index[:, None] == slots[None, :]).astype(BF16)]
    broadcast_in_dim x1 -> x0, local copies, waits for them, and re-layouts: 1.36 us -> none  [shards(): lengths = jnp.broadcast_to(cache_fill_length[:, None], (rows, LANES))]
    pallas_call x1, Pallas kernels: 96.6 us -> 95.5 us  [shards(): pl.pallas_call(kernel, out_shape=jax.ShapeDtypeStruct((rows, out_half), B...]
    unnamed x2 -> x1, local copies, waits for them, and re-layouts: 2.65 us -> 1.88 us
where the time goes in v2:
time: 97.6 us; the launch traced here: 97.3 us
  Pallas kernels  95.5 us (98%)
  local copies, waits for them, and re-layouts  1.88 us (2%)
    pallas_call x1, Pallas kernels, shards(): pl.pallas_call(kernel, out_shape=jax.ShapeDtypeStruct((rows, out_half), B...  95.5 us

profile of v2, /device:TPU:0, one launch (start us, length us, event | category | flops | bytes accessed | tf_op | source)
XLA Modules:
  0.0 97.3 jit_solution(3839535647066023124)
XLA Ops:
  0.0 95.5 %shard_map.145 = bf16[128,2048]{1,0:T(8,128)(2,1)} custom-call(s32[1,128]{1,0:T(1,128)} %bitcast.3, s32[1,128]{1,0:T(1,128)} %bitcast.4, s32[1,128]{1,0:T(1,128)} %bitcast.5, f32[8,32]{1,0:T(8,128)} %scales.1, bf16[128,4096]{1,0:T(8,128)(2,1)} %hidden.1, bf16[128,1024]{1,0:T(8,128)(2,1)} %base_q.1, bf16[128,1024]{1,0:T(8,128)(2,1)} %key_in.1, ...), custom_call_target="tpu_custom_call" | custom-call | tf_op jit(solution)/shard_map/pallas_call | solution.py:406
  95.5 1.9 %copy.17 = bf16[128,2048]{1,0:T(8,128)(2,1)} copy(bf16[128,2048]{1,0:T(8,128)(2,1)} %shard_map.145) | data formatting | bytes 1048576

commit v3 on v2

--- a/solution.py
+++ b/solution.py
@@ -12,8 +12,8 @@
 BLOCK = 128
 LANES = 128
 GROUPS = 2
-OUT_CHUNKS = 2
-ROW_BLOCK = 32
+OUT_CHUNKS = 1
+ROW_BLOCK = 64
 SUB = 16
 F32 = jnp.float32
 BF16 = jnp.bfloat16
@@ -251,9 +251,7 @@
             x_recv[h, :, :, :half].reshape(part, half), down_v[...].reshape(spread2, half)
         )
         mixed_v[h] = sum_cores(h, shrink, mask)
-        correct(0, h)
-    for g in range(1, GROUPS):
-        for h in range(halves):
+        for g in range(GROUPS):
             correct(g, h)
 
     for index in range(3, 9):

time: 97.6 us -> 95.8 us (0.982); the launches traced: 97.3 us -> 94.5 us
  Pallas kernels: 95.5 us -> 92.6 us
    pallas_call x1, Pallas kernels: 95.5 us -> 92.6 us  [shards(): pl.pallas_call(kernel, out_shape=jax.ShapeDtypeStruct((rows, out_half), B...]
where the time goes in v3:
time: 95.8 us; the launch traced here: 94.5 us
  Pallas kernels  92.6 us (97%)
  local copies, waits for them, and re-layouts  1.88 us (2%)
    pallas_call x1, Pallas kernels, shards(): pl.pallas_call(kernel, out_shape=jax.ShapeDtypeStruct((rows, out_half), B...  92.6 us

profile of v3, /device:TPU:0, one launch (start us, length us, event | category | flops | bytes accessed | tf_op | source)
XLA Modules:
  0.0 94.5 jit_solution(15472829516189067193)
XLA Ops:
  0.0 92.6 %shard_map.145 = bf16[128,2048]{1,0:T(8,128)(2,1)} custom-call(s32[1,128]{1,0:T(1,128)} %bitcast.3, s32[1,128]{1,0:T(1,128)} %bitcast.4, s32[1,128]{1,0:T(1,128)} %bitcast.5, f32[8,32]{1,0:T(8,128)} %scales.1, bf16[128,4096]{1,0:T(8,128)(2,1)} %hidden.1, bf16[128,1024]{1,0:T(8,128)(2,1)} %base_q.1, bf16[128,1024]{1,0:T(8,128)(2,1)} %key_in.1, ...), custom_call_target="tpu_custom_call" | custom-call | tf_op jit(solution)/shard_map/pallas_call | solution.py:404
  92.6 1.9 %copy.17 = bf16[128,2048]{1,0:T(8,128)(2,1)} copy(bf16[128,2048]{1,0:T(8,128)(2,1)} %shard_map.145) | data formatting | bytes 1048576
